TPU v7x, 32 devices: a whole 2x2x4 slice. The times are simulated.
32 devices in a mesh: grp: 2 (over x), col: 16 (over z, y, core).
Axes of the slice: x: 2, y: 2, z: 4, core: 2. Of those that a mesh axis runs over, the one named last changes fastest.
Arguments:
- leaf_right_hand: float32 [320, 256, 128], P(('grp', 'col')), parts along dimension 0, may hold values from -6 to 6
- leaf_diagonal_inverse: bfloat16 [320, 256, 256], P(('grp', 'col')), parts along dimension 0, as said below
- leaf_coupling: bfloat16 [320, 4, 256, 256], P(('grp', 'col')), parts along dimension 0, may hold values from -0.03125 to 0.03125
- leaf_pattern: int32 [320, 4], P(('grp', 'col')), parts along dimension 0, may hold values 0 or 1
- top_rhs: float32 [32, 256, 128], P(('grp', 'col')), parts along dimension 0, may hold values from -6 to 6
- top_inverse: bfloat16 [32, 256, 256], P(('grp', 'col')), parts along dimension 0, as said below
- top_coupling: bfloat16 [32, 4, 256, 256], P(('grp', 'col')), parts along dimension 0, may hold values from -0.09375 to 0.09375
Outputs:
- leaf_solution: float32 [320, 256, 128], P(('grp', 'col')), parts along dimension 0
- top_solution: float32 [32, 256, 128], P(('grp', 'col')), parts along dimension 0
There are 2 independent parts, one for each index of `grp`. A program takes and returns all parts, laid end to end along the dimension named above; each array names one. Nothing has to cross between parts.
Inputs may be any that keep to these rules, and one draw needn't show every extreme that they name: `leaf_diagonal_inverse`: lower triangular, diagonal between 0.7 and 1.3. `top_inverse`: lower triangular, diagonal between 0.7 and 1.3.
All inputs are finite; a program needn't handle non-finite values. No bound on the sum of `leaf_pattern` on one device may be relied on, other than what follows from the above.
Results may differ from a plain program's by a relative error of at most 0.0044.
Values sent between devices are 32-bit elements; how exact they have to be, the bound alone decides.
A program may use at most 64 MiB of HBM per device.

v0:
```python
import jax
import jax.numpy as jnp
from jax import lax
from jax.sharding import PartitionSpec as P


def from_partner(shard, axis, distance):
    return lax.ppermute(shard, axis, [(i, i ^ 1 << distance) for i in range(lax.axis_size(axis))])


def rounded_result(value):
    return value.astype(jnp.bfloat16)


def local(
    leaf_right_hand,
    leaf_diagonal_inverse,
    leaf_coupling,
    leaf_pattern,
    top_rhs,
    top_inverse,
    top_coupling,
):
    count = lax.axis_size("col")
    depth = count.bit_length() - 1
    device = lax.axis_index("col")
    bit_values = device >> jnp.arange(depth, dtype=jnp.int32) & 1
    trailing = jnp.sum(jnp.cumprod(bit_values))
    own_level = depth - 1 - trailing
    mask_values = leaf_pattern.astype(jnp.bfloat16)[:, :, None, None]
    leaf_forward = jnp.einsum(
        "efj,ejs->efs",
        leaf_diagonal_inverse,
        rounded_result(leaf_right_hand),
        preferred_element_type=jnp.float32,
    )
    masked = mask_values * rounded_result(leaf_forward)[:, None]
    leaf_terms = jnp.einsum(
        "ikab,ikbr->kar", leaf_coupling, masked, preferred_element_type=jnp.float32
    )
    inverse_own = top_inverse[0]
    coupling_own = top_coupling[0]
    rhs_own = top_rhs[0]
    zeros_block = jnp.zeros_like(rhs_own)
    forward_own = zeros_block
    partial_terms = leaf_terms
    for level in reversed(range(depth)):
        total = partial_terms[level]
        for bit in range(depth - level):
            total = total + from_partner(total, "col", bit)
        owner_here = own_level == level
        solved = jnp.dot(
            inverse_own, rounded_result(rhs_own - total), preferred_element_type=jnp.float32
        )
        forward_own = jnp.where(owner_here, solved, forward_own)
        if level > 0:
            upward = jnp.einsum(
                "kab,br->kar",
                coupling_own[:level],
                rounded_result(solved),
                preferred_element_type=jnp.float32,
            )
            partial_terms = partial_terms[:level] + jnp.where(owner_here, upward, 0.0)
    backward_own = zeros_block
    columns = []
    for level in range(depth):
        owner_here = own_level == level
        carried_value = zeros_block
        if level > 0:
            known = jnp.stack(columns)
            carried_value = jnp.einsum(
                "kab,kar->br",
                coupling_own[:level],
                rounded_result(known),
                preferred_element_type=jnp.float32,
            )
        solved = jnp.einsum(
            "ab,ar->br",
            inverse_own,
            rounded_result(forward_own - carried_value),
            preferred_element_type=jnp.float32,
        )
        backward_own = jnp.where(owner_here, solved, backward_own)
        spread_value = jnp.where(owner_here, solved, 0.0)
        for bit in range(depth - level):
            spread_value = spread_value + from_partner(spread_value, "col", bit)
        columns.append(spread_value)
    path_values = jnp.stack(columns)
    masked_path = mask_values * rounded_result(path_values)[None]
    carried_leaf = jnp.einsum(
        "ikab,ikar->ibr", leaf_coupling, masked_path, preferred_element_type=jnp.float32
    )
    leaf_solution = jnp.einsum(
        "vdu,vdo->vuo",
        leaf_diagonal_inverse,
        rounded_result(leaf_forward - carried_leaf),
        preferred_element_type=jnp.float32,
    )
    top_out = jnp.where(own_level >= 0, backward_own, path_values[0])[None]
    return (leaf_solution, top_out)


def solution(mesh):
    in_specs = (
        P(("grp", "col"), None, None),
        P(("grp", "col"), None, None),
        P(("grp", "col"), None, None, None),
        P(("grp", "col"), None),
        P(("grp", "col"), None, None),
        P(("grp", "col"), None, None),
        P(("grp", "col"), None, None, None),
    )
    out_specs = (P(("grp", "col"), None, None), P(("grp", "col"), None, None))
    return jax.shard_map(local, mesh=mesh, in_specs=in_specs, out_specs=out_specs, check_vma=False)
```

profile of v0, /device:TPU:7, one launch (start us, length us, event | category | flops | bytes accessed | tf_op | source)
XLA Modules:
  0.0 99.8 jit_solution(17437780608173122712)
XLA Ops:
  2.0 2.9 %fusion.119 = (bf16[10,256,128]{2,1,0:T(8,128)(2,1)S(1)}, f32[10,256,128]{2,1,0:T(8,128)}) fusion(bf16[10,256,256]{2,1,0:T(8,128)(2,1)S(1)} %copy-done, f32[10,256,128]{2,1,0:T(8,128)} %param.7), kind=kOutput, calls=%fused_computation.107 | convolution fusion | flops 168427520 | bytes 4587520 | tf_op jit(solution)/shard_map/efj,ejs->efs/dot_general | solution.py:31
  5.1 4.4 %fusion.29 = f32[4,256,128]{1,2,0:T(8,128)S(1)} fusion(bf16[10,4,256,256]{3,2,1,0:T(8,128)(2,1)} %param.9, bf16[10,256,128]{1,2,0:T(8,128)(2,1)S(1)} %copy.16, bf16[10,4]{0,1:T(4,128)(2,1)S(1)} %convert_element_type.60), kind=kOutput, calls=%fused_computation.14 | convolution fusion | flops 672399360 | bytes 6422608 | tf_op jit(solution)/shard_map/ikab,ikbr->kar/dot_general | solution.py:38
  14.1 4.7 %collective-permute-done.2 = f32[256,128]{0,1:T(8,128)S(1)} collective-permute-done((f32[256,128]{0,1:T(8,128)S(1)}, f32[256,128]{0,1:T(8,128)S(1)}, u32[]{:S(2)}, u32[]{:S(2)}) %collective-permute-start.2) | collective-permute-done | bytes 131104 | tf_op jit(solution)/shard_map/ppermute | solution.py:8
  21.6 4.5 %collective-permute-done.4 = f32[256,128]{0,1:T(8,128)S(1)} collective-permute-done((f32[256,128]{0,1:T(8,128)S(1)}, f32[256,128]{0,1:T(8,128)S(1)}, u32[]{:S(2)}, u32[]{:S(2)}) %collective-permute-start.4) | collective-permute-done | bytes 131104 | tf_op jit(solution)/shard_map/ppermute | solution.py:8
  26.1 1.4 %collective-permute-start.5 = (f32[256,128]{0,1:T(8,128)S(1)}, f32[256,128]{0,1:T(8,128)S(1)}, u32[]{:S(2)}, u32[]{:S(2)}) collective-permute-start(f32[256,128]{0,1:T(8,128)S(1)} %add.75), channel_id=1, source_target_pairs={{0,4},{1,5},{2,6},{3,7},{4,0},{5,1},{6,2},{7,3},{8,12},{9,13},{10,... | collective-permute-start | bytes 393224 | tf_op jit(solution)/shard_map/ppermute | solution.py:8
  27.5 2.5 %collective-permute-done.5 = f32[256,128]{0,1:T(8,128)S(1)} collective-permute-done((f32[256,128]{0,1:T(8,128)S(1)}, f32[256,128]{0,1:T(8,128)S(1)}, u32[]{:S(2)}, u32[]{:S(2)}) %collective-permute-start.5) | collective-permute-done | bytes 131104 | tf_op jit(solution)/shard_map/ppermute | solution.py:8
  30.4 2.4 %collective-permute-start.6 = (f32[256,128]{0,1:T(8,128)S(1)}, f32[256,128]{0,1:T(8,128)S(1)}, u32[]{:S(2)}, u32[]{:S(2)}) collective-permute-start(f32[256,128]{0,1:T(8,128)S(1)} %fusion.41), channel_id=1, source_target_pairs={{0,1},{1,0},{2,3},{3,2},{4,5},{5,4},{6,7},{7,6},{8,9},{9,8},{10,11... | collective-permute-start | bytes 393224 | tf_op jit(solution)/shard_map/ppermute | solution.py:8
  34.1 4.5 %collective-permute-done.7 = f32[256,128]{0,1:T(8,128)S(1)} collective-permute-done((f32[256,128]{0,1:T(8,128)S(1)}, f32[256,128]{0,1:T(8,128)S(1)}, u32[]{:S(2)}, u32[]{:S(2)}) %collective-permute-start.7) | collective-permute-done | bytes 131104 | tf_op jit(solution)/shard_map/ppermute | solution.py:8
  38.6 1.4 %collective-permute-start.8 = (f32[256,128]{0,1:T(8,128)S(1)}, f32[256,128]{0,1:T(8,128)S(1)}, u32[]{:S(2)}, u32[]{:S(2)}) collective-permute-start(f32[256,128]{0,1:T(8,128)S(1)} %add.79), channel_id=1, source_target_pairs={{0,4},{1,5},{2,6},{3,7},{4,0},{5,1},{6,2},{7,3},{8,12},{9,13},{10,... | collective-permute-start | bytes 393224 | tf_op jit(solution)/shard_map/ppermute | solution.py:8
  40.0 2.5 %collective-permute-done.8 = f32[256,128]{0,1:T(8,128)S(1)} collective-permute-done((f32[256,128]{0,1:T(8,128)S(1)}, f32[256,128]{0,1:T(8,128)S(1)}, u32[]{:S(2)}, u32[]{:S(2)}) %collective-permute-start.8) | collective-permute-done | bytes 131104 | tf_op jit(solution)/shard_map/ppermute | solution.py:8
  42.5 2.4 %collective-permute-start.9 = (f32[256,128]{0,1:T(8,128)S(1)}, f32[256,128]{0,1:T(8,128)S(1)}, u32[]{:S(2)}, u32[]{:S(2)}) collective-permute-start(f32[256,128]{0,1:T(8,128)S(1)} %add.80), channel_id=1, source_target_pairs={{0,8},{1,9},{2,10},{3,11},{4,12},{5,13},{6,14},{7,15},{8,0},{9,1},... | collective-permute-start | bytes 393224 | tf_op jit(solution)/shard_map/ppermute | solution.py:8
  44.9 3.8 %collective-permute-done.9 = f32[256,128]{0,1:T(8,128)S(1)} collective-permute-done((f32[256,128]{0,1:T(8,128)S(1)}, f32[256,128]{0,1:T(8,128)S(1)}, u32[]{:S(2)}, u32[]{:S(2)}) %collective-permute-start.9) | collective-permute-done | bytes 131104 | tf_op jit(solution)/shard_map/ppermute | solution.py:8
  49.1 3.6 %collective-permute-start.10 = (f32[256,128]{0,1:T(8,128)S(1)}, f32[256,128]{0,1:T(8,128)S(1)}, u32[]{:S(2)}, u32[]{:S(2)}) collective-permute-start(f32[256,128]{0,1:T(8,128)S(1)} %fusion.38), channel_id=1, source_target_pairs={{0,1},{1,0},{2,3},{3,2},{4,5},{5,4},{6,7},{7,6},{8,9},{9,8},{10,11... | collective-permute-start | bytes 393224 | tf_op jit(solution)/shard_map/ppermute | solution.py:8
  54.0 4.5 %collective-permute-done.11 = f32[256,128]{0,1:T(8,128)S(1)} collective-permute-done((f32[256,128]{0,1:T(8,128)S(1)}, f32[256,128]{0,1:T(8,128)S(1)}, u32[]{:S(2)}, u32[]{:S(2)}) %collective-permute-start.11) | collective-permute-done | bytes 131104 | tf_op jit(solution)/shard_map/ppermute | solution.py:8
  58.9 3.4 %collective-permute-done.12 = f32[256,128]{0,1:T(8,128)S(1)} collective-permute-done((f32[256,128]{0,1:T(8,128)S(1)}, f32[256,128]{0,1:T(8,128)S(1)}, u32[]{:S(2)}, u32[]{:S(2)}) %collective-permute-start.12) | collective-permute-done | bytes 131104 | tf_op jit(solution)/shard_map/ppermute | solution.py:8
  62.4 2.1 %collective-permute-start.13 = (f32[256,128]{0,1:T(8,128)S(1)}, f32[256,128]{0,1:T(8,128)S(1)}, u32[]{:S(2)}, u32[]{:S(2)}) collective-permute-start(f32[256,128]{0,1:T(8,128)S(1)} %add.84), channel_id=1, source_target_pairs={{0,8},{1,9},{2,10},{3,11},{4,12},{5,13},{6,14},{7,15},{8,0},{9,1},... | collective-permute-start | bytes 393224 | tf_op jit(solution)/shard_map/ppermute | solution.py:8
  64.5 4.1 %collective-permute-done.13 = f32[256,128]{0,1:T(8,128)S(1)} collective-permute-done((f32[256,128]{0,1:T(8,128)S(1)}, f32[256,128]{0,1:T(8,128)S(1)}, u32[]{:S(2)}, u32[]{:S(2)}) %collective-permute-start.13) | collective-permute-done | bytes 131104 | tf_op jit(solution)/shard_map/ppermute | solution.py:8
  68.9 3.6 %collective-permute-start.14 = (f32[256,128]{0,1:T(8,128)S(1)}, f32[256,128]{0,1:T(8,128)S(1)}, u32[]{:S(2)}, u32[]{:S(2)}) collective-permute-start(f32[256,128]{0,1:T(8,128)S(1)} %get-tuple-element.12), channel_id=1, source_target_pairs={{0,1},{1,0},{2,3},{3,2},{4,5},{5,4},{6,7},{7,6},{8,9},{9,8},{10,11... | collective-permute-start | bytes 393224 | tf_op jit(solution)/shard_map/ppermute | solution.py:8
  73.8 4.5 %collective-permute-done.15 = f32[256,128]{0,1:T(8,128)S(1)} collective-permute-done((f32[256,128]{0,1:T(8,128)S(1)}, f32[256,128]{0,1:T(8,128)S(1)}, u32[]{:S(2)}, u32[]{:S(2)}) %collective-permute-start.15) | collective-permute-done | bytes 131104 | tf_op jit(solution)/shard_map/ppermute | solution.py:8
  78.5 3.7 %collective-permute-done.16 = f32[256,128]{0,1:T(8,128)S(1)} collective-permute-done((f32[256,128]{0,1:T(8,128)S(1)}, f32[256,128]{0,1:T(8,128)S(1)}, u32[]{:S(2)}, u32[]{:S(2)}) %collective-permute-start.16) | collective-permute-done | bytes 131104 | tf_op jit(solution)/shard_map/ppermute | solution.py:8
  82.5 2.4 %collective-permute-start.17 = (f32[256,128]{0,1:T(8,128)S(1)}, f32[256,128]{0,1:T(8,128)S(1)}, u32[]{:S(2)}, u32[]{:S(2)}) collective-permute-start(f32[256,128]{0,1:T(8,128)S(1)} %get-tuple-element.14), channel_id=1, source_target_pairs={{0,1},{1,0},{2,3},{3,2},{4,5},{5,4},{6,7},{7,6},{8,9},{9,8},{10,11... | collective-permute-start | bytes 393224 | tf_op jit(solution)/shard_map/ppermute | solution.py:8
  86.2 4.5 %collective-permute-done.18 = f32[256,128]{0,1:T(8,128)S(1)} collective-permute-done((f32[256,128]{0,1:T(8,128)S(1)}, f32[256,128]{0,1:T(8,128)S(1)}, u32[]{:S(2)}, u32[]{:S(2)}) %collective-permute-start.18) | collective-permute-done | bytes 131104 | tf_op jit(solution)/shard_map/ppermute | solution.py:8
  93.4 5.0 %convolution_bitcast_fusion = f32[10,256,128]{1,2,0:T(8,128)S(1)} fusion(bf16[10,256,256]{2,1,0:T(8,128)(2,1)S(1)} %copy-done, f32[10,256,128]{2,1,0:T(8,128)} %get-tuple-element.11, bf16[10,4,256,256]{3,2,1,0:T(8,128)(2,1)} %param.9, bf16[4,256,128]{1,2,0:T(8,128)(2,1)S(1)} %pad_maximum_fusion, bf16[10,4]{0,1:T(4,128)(2,1)S(1)} %convert_element_type.60), kind=kOutput, calls=%fused_computation.6 | convolution fusion | flops 840826880 | bytes 9437264 | tf_op jit(solution)/shard_map/vdu,vdo->vuo/dot_general | solution.py:93
  98.4 1.5 %copy.19 = f32[10,256,128]{2,1,0:T(8,128)} copy(f32[10,256,128]{1,2,0:T(8,128)S(1)} %convolution_bitcast_fusion) | data formatting | bytes 2621440
  (66 shorter events, 18.2 us)
Async XLA Ops:
  0.6 1.3 %copy-start = (bf16[10,256,256]{2,1,0:T(8,128)(2,1)S(1)}, bf16[10,256,256]{2,1,0:T(8,128)(2,1)}, u32[]{:S(2)}) copy-start(bf16[10,256,256]{2,1,0:T(8,128)(2,1)} %param.8) | copy-start | bytes 3932164
  5.1 6.6 %copy-start.3 = (f32[1,256,128]{2,1,0:T(8,128)S(1)}, f32[1,256,128]{2,1,0:T(8,128)}, u32[]{:S(2)}) copy-start(f32[1,256,128]{2,1,0:T(8,128)} %param.11) | copy-start | bytes 393220
  5.1 6.8 %copy-start.1 = (bf16[1,256,256]{2,1,0:T(8,128)(2,1)S(1)}, bf16[1,256,256]{2,1,0:T(8,128)(2,1)}, u32[]{:S(2)}) copy-start(bf16[1,256,256]{2,1,0:T(8,128)(2,1)} %param.12) | copy-start | bytes 393220
  9.5 2.6 %copy-start.2 = (bf16[1,4,256,256]{3,2,1,0:T(8,128)(2,1)S(1)}, bf16[1,4,256,256]{3,2,1,0:T(8,128)(2,1)}, u32[]{:S(2)}) copy-start(bf16[1,4,256,256]{3,2,1,0:T(8,128)(2,1)} %param.13) | copy-start | bytes 1572868
  9.5 2.3 %collective-permute-start = (f32[256,128]{0,1:T(8,128)S(1)}, f32[256,128]{0,1:T(8,128)S(1)}, u32[]{:S(2)}, u32[]{:S(2)}) collective-permute-start(f32[256,128]{0,1:T(8,128)S(1)} %slice_bitcast_fusion.2), channel_id=1, source_target_pairs={{0,1},{1,0},{2,3},{3,2},{4,5},{5,4},{6,7},{7,6},{8,9},{9,8},{10,11... | collective-permute-start | bytes 393224 | tf_op jit(solution)/shard_map/ppermute | solution.py:8
  12.4 1.4 %collective-permute-start.1 = (f32[256,128]{0,1:T(8,128)S(1)}, f32[256,128]{0,1:T(8,128)S(1)}, u32[]{:S(2)}, u32[]{:S(2)}) collective-permute-start(f32[256,128]{0,1:T(8,128)S(1)} %slice_bitcast_fusion.1), channel_id=1, source_target_pairs={{0,1},{1,0},{2,3},{3,2},{4,5},{5,4},{6,7},{7,6},{8,9},{9,8},{10,11... | collective-permute-start | bytes 393224 | tf_op jit(solution)/shard_map/ppermute | solution.py:8
  13.8 5.0 %collective-permute-start.2 = (f32[256,128]{0,1:T(8,128)S(1)}, f32[256,128]{0,1:T(8,128)S(1)}, u32[]{:S(2)}, u32[]{:S(2)}) collective-permute-start(f32[256,128]{0,1:T(8,128)S(1)} %fusion.117), channel_id=1, source_target_pairs={{0,2},{1,3},{2,0},{3,1},{4,6},{5,7},{6,4},{7,5},{8,10},{9,11},{10,... | collective-permute-start | bytes 393224 | tf_op jit(solution)/shard_map/ppermute | solution.py:8
  19.3 2.0 %collective-permute-start.3 = (f32[256,128]{0,1:T(8,128)S(1)}, f32[256,128]{0,1:T(8,128)S(1)}, u32[]{:S(2)}, u32[]{:S(2)}) collective-permute-start(f32[256,128]{0,1:T(8,128)S(1)} %slice_bitcast_fusion), channel_id=1, source_target_pairs={{0,1},{1,0},{2,3},{3,2},{4,5},{5,4},{6,7},{7,6},{8,9},{9,8},{10,11... | collective-permute-start | bytes 393224 | tf_op jit(solution)/shard_map/ppermute | solution.py:8
  21.3 4.8 %collective-permute-start.4 = (f32[256,128]{0,1:T(8,128)S(1)}, f32[256,128]{0,1:T(8,128)S(1)}, u32[]{:S(2)}, u32[]{:S(2)}) collective-permute-start(f32[256,128]{0,1:T(8,128)S(1)} %fusion.118), channel_id=1, source_target_pairs={{0,2},{1,3},{2,0},{3,1},{4,6},{5,7},{6,4},{7,5},{8,10},{9,11},{10,... | collective-permute-start | bytes 393224 | tf_op jit(solution)/shard_map/ppermute | solution.py:8
  26.1 3.9 %collective-permute-start.5 = (f32[256,128]{0,1:T(8,128)S(1)}, f32[256,128]{0,1:T(8,128)S(1)}, u32[]{:S(2)}, u32[]{:S(2)}) collective-permute-start(f32[256,128]{0,1:T(8,128)S(1)} %add.75), channel_id=1, source_target_pairs={{0,4},{1,5},{2,6},{3,7},{4,0},{5,1},{6,2},{7,3},{8,12},{9,13},{10,... | collective-permute-start | bytes 393224 | tf_op jit(solution)/shard_map/ppermute | solution.py:8
  30.4 3.4 %collective-permute-start.6 = (f32[256,128]{0,1:T(8,128)S(1)}, f32[256,128]{0,1:T(8,128)S(1)}, u32[]{:S(2)}, u32[]{:S(2)}) collective-permute-start(f32[256,128]{0,1:T(8,128)S(1)} %fusion.41), channel_id=1, source_target_pairs={{0,1},{1,0},{2,3},{3,2},{4,5},{5,4},{6,7},{7,6},{8,9},{9,8},{10,11... | collective-permute-start | bytes 393224 | tf_op jit(solution)/shard_map/ppermute | solution.py:8
  33.8 4.8 %collective-permute-start.7 = (f32[256,128]{0,1:T(8,128)S(1)}, f32[256,128]{0,1:T(8,128)S(1)}, u32[]{:S(2)}, u32[]{:S(2)}) collective-permute-start(f32[256,128]{0,1:T(8,128)S(1)} %add.78), channel_id=1, source_target_pairs={{0,2},{1,3},{2,0},{3,1},{4,6},{5,7},{6,4},{7,5},{8,10},{9,11},{10,... | collective-permute-start | bytes 393224 | tf_op jit(solution)/shard_map/ppermute | solution.py:8
  38.6 3.9 %collective-permute-start.8 = (f32[256,128]{0,1:T(8,128)S(1)}, f32[256,128]{0,1:T(8,128)S(1)}, u32[]{:S(2)}, u32[]{:S(2)}) collective-permute-start(f32[256,128]{0,1:T(8,128)S(1)} %add.79), channel_id=1, source_target_pairs={{0,4},{1,5},{2,6},{3,7},{4,0},{5,1},{6,2},{7,3},{8,12},{9,13},{10,... | collective-permute-start | bytes 393224 | tf_op jit(solution)/shard_map/ppermute | solution.py:8
  42.5 6.2 %collective-permute-start.9 = (f32[256,128]{0,1:T(8,128)S(1)}, f32[256,128]{0,1:T(8,128)S(1)}, u32[]{:S(2)}, u32[]{:S(2)}) collective-permute-start(f32[256,128]{0,1:T(8,128)S(1)} %add.80), channel_id=1, source_target_pairs={{0,8},{1,9},{2,10},{3,11},{4,12},{5,13},{6,14},{7,15},{8,0},{9,1},... | collective-permute-start | bytes 393224 | tf_op jit(solution)/shard_map/ppermute | solution.py:8
  49.1 4.6 %collective-permute-start.10 = (f32[256,128]{0,1:T(8,128)S(1)}, f32[256,128]{0,1:T(8,128)S(1)}, u32[]{:S(2)}, u32[]{:S(2)}) collective-permute-start(f32[256,128]{0,1:T(8,128)S(1)} %fusion.38), channel_id=1, source_target_pairs={{0,1},{1,0},{2,3},{3,2},{4,5},{5,4},{6,7},{7,6},{8,9},{9,8},{10,11... | collective-permute-start | bytes 393224 | tf_op jit(solution)/shard_map/ppermute | solution.py:8
  53.7 4.8 %collective-permute-start.11 = (f32[256,128]{0,1:T(8,128)S(1)}, f32[256,128]{0,1:T(8,128)S(1)}, u32[]{:S(2)}, u32[]{:S(2)}) collective-permute-start(f32[256,128]{0,1:T(8,128)S(1)} %add.82), channel_id=1, source_target_pairs={{0,2},{1,3},{2,0},{3,1},{4,6},{5,7},{6,4},{7,5},{8,10},{9,11},{10,... | collective-permute-start | bytes 393224 | tf_op jit(solution)/shard_map/ppermute | solution.py:8
  58.5 3.9 %collective-permute-start.12 = (f32[256,128]{0,1:T(8,128)S(1)}, f32[256,128]{0,1:T(8,128)S(1)}, u32[]{:S(2)}, u32[]{:S(2)}) collective-permute-start(f32[256,128]{0,1:T(8,128)S(1)} %add.83), channel_id=1, source_target_pairs={{0,4},{1,5},{2,6},{3,7},{4,0},{5,1},{6,2},{7,3},{8,12},{9,13},{10,... | collective-permute-start | bytes 393224 | tf_op jit(solution)/shard_map/ppermute | solution.py:8
  62.4 6.2 %collective-permute-start.13 = (f32[256,128]{0,1:T(8,128)S(1)}, f32[256,128]{0,1:T(8,128)S(1)}, u32[]{:S(2)}, u32[]{:S(2)}) collective-permute-start(f32[256,128]{0,1:T(8,128)S(1)} %add.84), channel_id=1, source_target_pairs={{0,8},{1,9},{2,10},{3,11},{4,12},{5,13},{6,14},{7,15},{8,0},{9,1},... | collective-permute-start | bytes 393224 | tf_op jit(solution)/shard_map/ppermute | solution.py:8
  68.9 4.5 %collective-permute-start.14 = (f32[256,128]{0,1:T(8,128)S(1)}, f32[256,128]{0,1:T(8,128)S(1)}, u32[]{:S(2)}, u32[]{:S(2)}) collective-permute-start(f32[256,128]{0,1:T(8,128)S(1)} %get-tuple-element.12), channel_id=1, source_target_pairs={{0,1},{1,0},{2,3},{3,2},{4,5},{5,4},{6,7},{7,6},{8,9},{9,8},{10,11... | collective-permute-start | bytes 393224 | tf_op jit(solution)/shard_map/ppermute | solution.py:8
  73.5 4.8 %collective-permute-start.15 = (f32[256,128]{0,1:T(8,128)S(1)}, f32[256,128]{0,1:T(8,128)S(1)}, u32[]{:S(2)}, u32[]{:S(2)}) collective-permute-start(f32[256,128]{0,1:T(8,128)S(1)} %add.86), channel_id=1, source_target_pairs={{0,2},{1,3},{2,0},{3,1},{4,6},{5,7},{6,4},{7,5},{8,10},{9,11},{10,... | collective-permute-start | bytes 393224 | tf_op jit(solution)/shard_map/ppermute | solution.py:8
  78.3 3.9 %collective-permute-start.16 = (f32[256,128]{0,1:T(8,128)S(1)}, f32[256,128]{0,1:T(8,128)S(1)}, u32[]{:S(2)}, u32[]{:S(2)}) collective-permute-start(f32[256,128]{0,1:T(8,128)S(1)} %add.87), channel_id=1, source_target_pairs={{0,4},{1,5},{2,6},{3,7},{4,0},{5,1},{6,2},{7,3},{8,12},{9,13},{10,... | collective-permute-start | bytes 393224 | tf_op jit(solution)/shard_map/ppermute | solution.py:8
  82.5 3.4 %collective-permute-start.17 = (f32[256,128]{0,1:T(8,128)S(1)}, f32[256,128]{0,1:T(8,128)S(1)}, u32[]{:S(2)}, u32[]{:S(2)}) collective-permute-start(f32[256,128]{0,1:T(8,128)S(1)} %get-tuple-element.14), channel_id=1, source_target_pairs={{0,1},{1,0},{2,3},{3,2},{4,5},{5,4},{6,7},{7,6},{8,9},{9,8},{10,11... | collective-permute-start | bytes 393224 | tf_op jit(solution)/shard_map/ppermute | solution.py:8
  85.9 4.8 %collective-permute-start.18 = (f32[256,128]{0,1:T(8,128)S(1)}, f32[256,128]{0,1:T(8,128)S(1)}, u32[]{:S(2)}, u32[]{:S(2)}) collective-permute-start(f32[256,128]{0,1:T(8,128)S(1)} %add.89), channel_id=1, source_target_pairs={{0,2},{1,3},{2,0},{3,1},{4,6},{5,7},{6,4},{7,5},{8,10},{9,11},{10,... | collective-permute-start | bytes 393224 | tf_op jit(solution)/shard_map/ppermute | solution.py:8
  91.1 2.2 %collective-permute-start.19 = (f32[256,128]{0,1:T(8,128)S(1)}, f32[256,128]{0,1:T(8,128)S(1)}, u32[]{:S(2)}, u32[]{:S(2)}) collective-permute-start(f32[256,128]{0,1:T(8,128)S(1)} %get-tuple-element.9), channel_id=1, source_target_pairs={{0,1},{1,0},{2,3},{3,2},{4,5},{5,4},{6,7},{7,6},{8,9},{9,8},{10,11... | collective-permute-start | bytes 393224 | tf_op jit(solution)/shard_map/ppermute | solution.py:8
where the time goes:
time: 101 us; the launch traced here: 99.8 us
  waiting for transfers between devices  53.9 us (53%)
  starting transfers between devices  24.6 us (24%)
  matrix products  14.8 us (15%)
  local copies, waits for them, and re-layouts  3.16 us (3%)
  other arithmetic  1.92 us (2%)
  between operations  1.53 us (2%)
    ppermute x20, waiting for transfers between devices, from_partner(): lax.ppermute(shard, axis, [(i, i ^ 1 << distance) for i in range(lax.axis...  53.9 us
    ppermute x20, starting transfers between devices, from_partner(): lax.ppermute(shard, axis, [(i, i ^ 1 << distance) for i in range(lax.axis...  24.6 us
    dot_general x1, matrix products, local(): jnp.einsum('vdu,vdo->vuo', leaf_diagonal_inverse, rounded_result(leaf_for...  4.95 us
    dot_general x1, matrix products, local(): jnp.einsum('ikab,ikbr->kar', leaf_coupling, masked, preferred_element_typ...  4.35 us
    unnamed x11, local copies, waits for them, and re-layouts  2.87 us
    dot_general x1, matrix products, local(): jnp.einsum('efj,ejs->efs', leaf_diagonal_inverse, rounded_result(leaf_rig...  2.86 us
  transfers between devices with their start and end apart: 20, of which 19 were waited for; matrix products, arithmetic and copies ran while one was open for 2% of the time, Pallas kernels for 0%

commit v1 on v0

v1 whole, which is shorter than its diff:
```python
import functools

import jax
import jax.numpy as jnp
from jax import lax
from jax.experimental import pallas as pl
from jax.experimental.pallas import tpu as pltpu
from jax.sharding import PartitionSpec as P

F32, BF16 = jnp.float32, jnp.bfloat16


def mm(a, b):
    return jnp.dot(a.astype(BF16), b.astype(BF16), preferred_element_type=F32)


def kernel(
    depth,
    rhs_hbm, dinv_hbm, coup_hbm, pat, trhs_hbm, tinv_hbm, tcoup_hbm,
    sol_hbm, top_hbm,
    rhs, dinv, coup, trhs, tinv, tcoup, fwd, fwd_t, out, top_out,
    terms, slots, stage, anc, path, own_x, y_t,
    in_sem, coup_sem, tin_sem, out_sem, top_sem,
    slot_sem, anc_sem, path_sem, part_send, up_send, down_send,
):
    leaves = rhs.shape[0]
    last = depth - 1
    me = lax.axis_index("col")
    even = lax.rem(me, 2) == 0
    odd = lax.rem(me, 2) == 1
    partner = jnp.where(even, me + 1, me - 1)

    def node(level):
        half = 1 << (last - level)
        is_node = lax.rem(me, 2 * half) == half - 1
        left = lax.rem((me + 1 - half) // (2 * half), 2) == 0
        parent = jnp.where(left, me + half, me - half)
        return is_node, left, parent, half // 2

    def load(src, dst, sem):
        return pltpu.make_async_copy(src, dst, sem)

    copy_rhs = load(rhs_hbm, rhs, in_sem.at[0])
    copy_dinv = load(dinv_hbm, dinv, in_sem.at[1])
    copy_coup = [load(coup_hbm.at[:, k], coup.at[:, k], coup_sem.at[k]) for k in range(depth)]
    copy_tinv = load(tinv_hbm, tinv, tin_sem.at[0])
    copy_trhs = load(trhs_hbm, trhs, tin_sem.at[1])
    copy_tcoup = load(tcoup_hbm, tcoup, tin_sem.at[2])
    copy_dinv.start()
    copy_rhs.start()
    copy_coup[last].start()
    copy_tinv.start()
    copy_trhs.start()
    for k in reversed(range(last)):
        copy_coup[k].start()
    copy_tcoup.start()

    barrier = pltpu.get_barrier_semaphore()

    def greet(device):
        pl.semaphore_signal(barrier, inc=1, device_id={"col": device}, device_id_type=pl.DeviceIdType.MESH)

    greet(partner)
    for level in range(depth):
        is_node, left, parent, quarter = node(level)

        @pl.when(is_node)
        def _():
            if level > 0:
                greet(parent)
            if level < last:
                greet(me - quarter)
                greet(me + quarter)

    def send(src, dst, send_sem, recv_sem, device):
        return pltpu.make_async_remote_copy(
            src_ref=src, dst_ref=dst, send_sem=send_sem, recv_sem=recv_sem,
            device_id={"col": device}, device_id_type=pl.DeviceIdType.MESH,
        )

    def part_copy(k):
        return send(terms.at[k], slots.at[0, k], part_send.at[k], slot_sem.at[0, k], partner)

    def up_copy(side, k, parent):
        return send(stage.at[k], slots.at[side, k], up_send.at[k], slot_sem.at[side, k], parent)

    def down_copy(src, side, k, child, to_even):
        dst, sem = (path, path_sem) if to_even else (anc, anc_sem)
        return send(src, dst.at[k], down_send.at[side, k], sem.at[k], child)

    def pair_copy(k):
        return send(path.at[k], path.at[k], down_send.at[0, k], path_sem.at[k], partner)

    def slot_wait(side, k):
        send(slots.at[side, k], slots.at[side, k], part_send.at[k], slot_sem.at[side, k], partner).wait_recv()

    def anc_wait(k):
        send(anc.at[k], anc.at[k], part_send.at[k], anc_sem.at[k], partner).wait_recv()

    def path_wait(k):
        send(path.at[k], path.at[k], part_send.at[k], path_sem.at[k], partner).wait_recv()

    copy_dinv.wait()
    copy_rhs.wait()
    unroll = max(u for u in range(1, 6) if leaves % u == 0)

    def over_leaves(body):
        def block(b, carry):
            for u in range(unroll):
                body(b * unroll + u)
            return carry
        lax.fori_loop(0, leaves // unroll, block, 0)

    def leaf_solve(i):
        fwd[i] = mm(dinv[i], rhs[i])

    over_leaves(leaf_solve)

    def leaf_term(k):
        copy_coup[k].wait()

        def block(b, acc):
            for u in range(unroll):
                i = b * unroll + u
                acc = acc + pat[i, k].astype(F32) * mm(coup[i, k], fwd[i])
            return acc

        terms[k] = lax.fori_loop(0, leaves // unroll, block, jnp.zeros(terms.shape[1:], F32))

    def flip(i):
        fwd_t[i] = fwd[i].T

    leaf_term(last)
    count = 1
    for level in range(depth):
        is_node = node(level)[0]
        mine = (1 if level > 0 else 0) + (2 if level < last else 0)
        count = count + jnp.where(is_node, mine, 0)
    pl.semaphore_wait(barrier, count)

    @pl.when(odd)
    def _():
        part_copy(last).start()

    for k in reversed(range(last)):
        leaf_term(k)

        @pl.when(odd)
        def _():
            part_copy(k).start()

    copy_tinv.wait()
    copy_trhs.wait()
    copy_tcoup.wait()

    @pl.when(odd)
    def _():
        over_leaves(flip)

    for level in reversed(range(depth)):
        is_node, left, parent, quarter = node(level)

        @pl.when(is_node)
        def _():
            def rest(k):
                slot_wait(0, k)
                if level == last:
                    return terms[k] + slots[0, k]
                slot_wait(1, k)
                return slots[0, k] + slots[1, k]

            y = mm(tinv[0], trhs[0] - rest(level))
            for k in reversed(range(level)):
                stage[k] = rest(k) + mm(tcoup[0, k], y)

                @pl.when(left)
                def _():
                    up_copy(0, k, parent).start()

                @pl.when(jnp.logical_not(left))
                def _():
                    up_copy(1, k, parent).start()

            y_t[...] = y.T

    @pl.when(even)
    def _():
        over_leaves(flip)

    def leaf_back(k):
        x = path[k].astype(BF16)

        def body(i):
            value = fwd_t[i] - pat[i, k].astype(F32) * mm(x, coup[i, k])
            if k < last:
                fwd_t[i] = value
            else:
                out[i] = mm(value, dinv[i]).T
                pltpu.make_async_copy(out.at[i], sol_hbm.at[i], out_sem.at[i]).start()

        over_leaves(body)

    for level in range(last):
        is_node, left, parent, quarter = node(level)

        @pl.when(is_node)
        def _():
            value = y_t[...]
            to_even = level + 1 == last
            for k in range(level):
                anc_wait(k)
                down_copy(anc.at[k], 0, k, me - quarter, to_even).start()
                down_copy(anc.at[k], 1, k, me + quarter, to_even).start()
                value = value - mm(anc[k], tcoup[0, k])
            own_x[...] = mm(value, tinv[0])
            down_copy(own_x, 0, level, me - quarter, to_even).start()
            down_copy(own_x, 1, level, me + quarter, to_even).start()
            top_out[0] = own_x[...].T

    @pl.when(even)
    def _():
        for k in range(last):
            path_wait(k)
            pair_copy(k).start()
            y_t[...] = y_t[...] - mm(path[k], tcoup[0, k])
            if k + 1 == last:
                path[last] = mm(y_t[...], tinv[0])
                pair_copy(last).start()
            leaf_back(k)
        top_out[0] = path[last].T

    @pl.when(odd)
    def _():
        for k in range(last):
            path_wait(k)
            leaf_back(k)
        path_wait(last)

    @pl.when(me == (1 << depth) - 1)
    def _():
        top_out[0] = path[0].T

    copy_top = pltpu.make_async_copy(top_out, top_hbm, top_sem)
    copy_top.start()
    leaf_back(last)

    @pl.when(odd)
    def _():
        for k in range(depth):
            part_copy(k).wait_send()

    for level in range(depth):
        is_node, left, parent, quarter = node(level)

        @pl.when(is_node)
        def _():
            for k in range(level):
                up_copy(0, k, parent).wait_send()
            if level < last:
                for k in range(level + 1):
                    down_copy(own_x, 0, k, partner, True).wait_send()
                    down_copy(own_x, 1, k, partner, True).wait_send()
            else:
                for k in range(depth):
                    pair_copy(k).wait_send()

    copy_top.wait()

    def out_wait(i):
        pltpu.make_async_copy(out.at[i], sol_hbm.at[i], out_sem.at[i]).wait()

    over_leaves(out_wait)


def local(leaf_right_hand, leaf_diagonal_inverse, leaf_coupling, leaf_pattern, top_rhs, top_inverse, top_coupling):
    depth = lax.axis_size("col").bit_length() - 1
    leaves, width, right = leaf_right_hand.shape
    tall, flat = (width, right), (right, width)
    anywhere = pl.BlockSpec(memory_space=pl.ANY)
    sem = pltpu.SemaphoreType.DMA
    return pl.pallas_call(
        functools.partial(kernel, depth),
        out_shape=(
            jax.ShapeDtypeStruct(leaf_right_hand.shape, F32),
            jax.ShapeDtypeStruct(top_rhs.shape, F32),
        ),
        in_specs=[anywhere] * 3 + [pl.BlockSpec(memory_space=pltpu.SMEM)] + [anywhere] * 3,
        out_specs=(anywhere, anywhere),
        scratch_shapes=[
            pltpu.VMEM(leaf_right_hand.shape, F32),
            pltpu.VMEM(leaf_diagonal_inverse.shape, BF16),
            pltpu.VMEM(leaf_coupling.shape, BF16),
            pltpu.VMEM(top_rhs.shape, F32),
            pltpu.VMEM(top_inverse.shape, BF16),
            pltpu.VMEM(top_coupling.shape, BF16),
            pltpu.VMEM((leaves, *tall), F32),
            pltpu.VMEM((leaves, *flat), F32),
            pltpu.VMEM((leaves, *tall), F32),
            pltpu.VMEM((1, *tall), F32),
            pltpu.VMEM((depth, *tall), F32),
            pltpu.VMEM((2, depth, *tall), F32),
            pltpu.VMEM((depth, *tall), F32),
            pltpu.VMEM((depth, *flat), F32),
            pltpu.VMEM((depth, *flat), F32),
            pltpu.VMEM(flat, F32),
            pltpu.VMEM(flat, F32),
            sem((2,)), sem((depth,)), sem((3,)), sem((leaves,)), sem,
            sem((2, depth)), sem((depth,)), sem((depth,)), sem((depth,)), sem((depth,)), sem((2, depth)),
        ],
        compiler_params=pltpu.CompilerParams(
            collective_id=0, has_side_effects=True, vmem_limit_bytes=56 * 2**20
        ),
    )(leaf_right_hand, leaf_diagonal_inverse, leaf_coupling, leaf_pattern, top_rhs, top_inverse, top_coupling)


def solution(mesh):
    both = ("grp", "col")
    three, four = P(both, None, None), P(both, None, None, None)
    in_specs = (three, three, four, P(both, None), three, three, four)
    return jax.shard_map(local, mesh=mesh, in_specs=in_specs, out_specs=(three, three), check_vma=False)
```

time: 101 us -> 46.9 us (0.46)
  waiting for transfers between devices: 53.9 us -> 0 us
  Pallas kernels: 0 us -> 41.5 us
  starting transfers between devices: 24.6 us -> 0 us
  matrix products: 14.8 us -> 0 us
  other arithmetic: 1.92 us -> 0 us
  local copies, waits for them, and re-layouts: 3.16 us -> 4.53 us
    ppermute x20 -> x0, waiting for transfers between devices: 53.9 us -> none  [from_partner(): lax.ppermute(shard, axis, [(i, i ^ 1 << distance) for i in range(lax.axis...]
    pallas_call x0 -> x1, Pallas kernels: none -> 41.5 us  [local(): pl.pallas_call(functools.partial(kernel, depth), out_shape=(jax.ShapeDtyp...]
    ppermute x20 -> x0, starting transfers between devices: 24.6 us -> none  [from_partner(): lax.ppermute(shard, axis, [(i, i ^ 1 << distance) for i in range(lax.axis...]
    dot_general x14 -> x0, matrix products: 14.8 us -> none  [the longest x1 4.95 us: local(): jnp.einsum('vdu,vdo->vuo', leaf_diagonal_inverse, rounded_result(leaf_for...]
    unnamed x11 -> x5, local copies, waits for them, and re-layouts: 2.87 us -> 4.53 us
  transfers between devices with their start and end apart: 20 -> 0, of which waited for: 19 -> 0; matrix products, arithmetic and copies ran while one was open for 2% -> 0% of each run, Pallas kernels for 0% -> 0%
where the time goes in v1:
time: 46.9 us; the launch traced here: 46.7 us
  Pallas kernels  41.5 us (88%)
  local copies, waits for them, and re-layouts  4.53 us (10%)
  between operations  0.65 us (1%)
    pallas_call x1, Pallas kernels, local(): pl.pallas_call(functools.partial(kernel, depth), out_shape=(jax.ShapeDtyp...  41.5 us
    unnamed x5, local copies, waits for them, and re-layouts  4.53 us

profile of v1, /device:TPU:7, one launch (start us, length us, event | category | flops | bytes accessed | tf_op | source)
XLA Modules:
  0.0 46.7 jit_solution(13113245453178542933)
XLA Ops:
  0.6 1.4 %copy.9.pat = s32[10,4]{1,0:T(8,128)} copy(s32[10,4]{0,1:T(4,128)} %param.10) | data formatting | bytes 320 | tf_op args[3]
  2.0 41.5 %shard_map.86 = (f32[10,256,128]{2,1,0:T(8,128)}, f32[1,256,128]{2,1,0:T(8,128)}) custom-call(f32[10,256,128]{2,1,0:T(8,128)} %rhs_hbm.1, bf16[10,256,256]{2,1,0:T(8,128)(2,1)} %dinv_hbm.1, bf16[10,4,256,256]{3,2,1,0:T(8,128)(2,1)} %coup_hbm.1, s32[10,4]{1,0:T(8,128)} %copy.9.pat, f32[1,256,128]{2,1,0:T(8,128)} %trhs_hbm.1, bf16[1,256,256]{2,1,0:T(8,128)(2,1)} %tinv_hbm.1, ...), custom_call_target="tpu_custom_call" | custom-call | tf_op jit(solution)/shard_map/pallas_call | solution.py:281
  43.5 0.0 copy-start
  43.5 2.5 %copy.12 = f32[10,256,128]{2,1,0:T(8,128)} copy(f32[10,256,128]{2,1,0:T(8,128)} %get-tuple-element.4) | data formatting | bytes 2621440
  46.0 0.0 copy-done
  46.0 0.7 %copy.13 = f32[1,256,128]{2,1,0:T(8,128)} copy(f32[1,256,128]{2,1,0:T(8,128)S(1)} %copy-done) | data formatting | bytes 262144
Async XLA Ops:
  43.5 2.5 %copy-start = (f32[1,256,128]{2,1,0:T(8,128)S(1)}, f32[1,256,128]{2,1,0:T(8,128)}, u32[]{:S(2)}) copy-start(f32[1,256,128]{2,1,0:T(8,128)} %get-tuple-element.5) | copy-start | bytes 393220

commit v2 on v1

v2 whole, which is shorter than its diff:
```python
import functools

import jax
import jax.numpy as jnp
from jax import lax
from jax.experimental import pallas as pl
from jax.experimental.pallas import tpu as pltpu
from jax.sharding import PartitionSpec as P

F32, BF16 = jnp.float32, jnp.bfloat16


def mm(a, b):
    return jnp.dot(a.astype(BF16), b.astype(BF16), preferred_element_type=F32)


def kernel(
    depth,
    rhs_hbm, dinv_hbm, coup_hbm, pat, trhs_hbm, tinv_hbm, tcoup_hbm,
    sol_hbm, top_hbm,
    rhs, dinv, coup, trhs, tinv, tcoup, fwd, fwd_t, out, top_out,
    terms, slots, stage, path, y_t,
    own_mats, mats, high_rhs, mine, theirs, high_y, high_x,
    in_sem, coup_sem, tin_sem, out_sem, top_sem,
    slot_sem, path_sem, part_send, up_send, down_send,
    mat_send, mat_sem, rhs_sem, swap_send, swap_sem,
):
    leaves = rhs.shape[0]
    last = depth - 1
    hub_level = depth - 2
    me = lax.axis_index("col")
    even = lax.rem(me, 2) == 0
    odd = lax.rem(me, 2) == 1
    partner = jnp.where(even, me + 1, me - 1)
    is_hub = lax.rem(me, 4) == 1
    left = lax.rem(me, 4) == 0
    parent = jnp.where(left, me + 1, me - 1)

    def owner(level):
        span = 1 << (depth - level)
        return lax.rem(me, span) == span // 2 - 1

    def hubs(level):
        span = 1 << (depth - level)
        return [me + 1 - span // 2 + 4 * t + 1 for t in range(span // 4)]

    def owner_of(level):
        span = 1 << (depth - level)
        return me // span * span + span // 2 - 1

    def opposite(level):
        step = 4 << (hub_level - 1 - level)
        return jnp.where(lax.rem(me // step, 2) == 0, me + step, me - step)

    def load(src, dst, sem):
        return pltpu.make_async_copy(src, dst, sem)

    copy_rhs = load(rhs_hbm, rhs, in_sem.at[0])
    copy_dinv = load(dinv_hbm, dinv, in_sem.at[1])
    copy_coup = [load(coup_hbm.at[:, k], coup.at[:, k], coup_sem.at[k]) for k in range(depth)]
    copy_tinv = load(tinv_hbm, tinv, tin_sem.at[0])
    copy_trhs = load(trhs_hbm, trhs, tin_sem.at[1])
    copy_tcoup = load(tcoup_hbm, tcoup, tin_sem.at[2])
    copy_tinv.start()
    copy_trhs.start()
    copy_tcoup.start()
    copy_dinv.start()
    copy_rhs.start()
    for k in reversed(range(depth)):
        copy_coup[k].start()

    barrier = pltpu.get_barrier_semaphore()

    def greet(device):
        pl.semaphore_signal(barrier, inc=1, device_id={"col": device}, device_id_type=pl.DeviceIdType.MESH)

    greet(partner)

    @pl.when(even)
    def _():
        greet(parent)

    @pl.when(is_hub)
    def _():
        greet(me - 1)
        greet(me + 1)
        for level in range(hub_level):
            greet(owner_of(level))
            greet(opposite(level))

    count = 1 + jnp.where(even, 1, 0) + jnp.where(is_hub, 2 + 2 * hub_level, 0)
    for level in range(hub_level):

        @pl.when(owner(level))
        def _():
            for hub in hubs(level):
                greet(hub)

        count = count + jnp.where(owner(level), 1 << (hub_level - level), 0)

    def send(src, dst, send_sem, recv_sem, device):
        return pltpu.make_async_remote_copy(
            src_ref=src, dst_ref=dst, send_sem=send_sem, recv_sem=recv_sem,
            device_id={"col": device}, device_id_type=pl.DeviceIdType.MESH,
        )

    def part_copy(k):
        return send(terms.at[k], slots.at[0, k], part_send.at[k], slot_sem.at[0, k], partner)

    def up_copy(side, k):
        return send(stage.at[k], slots.at[side, k], up_send.at[k], slot_sem.at[side, k], parent)

    def down_copy(src, side, k, child):
        return send(src, path.at[k], down_send.at[side, k], path_sem.at[k], child)

    def pair_copy(k):
        return send(path.at[k], path.at[k], down_send.at[0, k], path_sem.at[k], partner)

    def swap_copy(level, k):
        return send(mine.at[level, k], theirs.at[level, k], swap_send.at[level, k], swap_sem.at[level, k], opposite(level))

    def mat_copy(level, k, t, hub):
        return send(own_mats.at[k], mats.at[level, k], mat_send.at[t, k], mat_sem.at[level, k], hub)

    def rhs_copy(level, t, hub):
        return send(trhs.at[0], high_rhs.at[level], mat_send.at[t, hub_level], rhs_sem.at[level], hub)

    def slot_wait(side, k):
        send(slots.at[side, k], slots.at[side, k], part_send.at[k], slot_sem.at[side, k], partner).wait_recv()

    def path_wait(k):
        send(path.at[k], path.at[k], part_send.at[k], path_sem.at[k], partner).wait_recv()

    copy_tinv.wait()
    copy_trhs.wait()
    copy_tcoup.wait()
    copy_dinv.wait()
    copy_rhs.wait()
    unroll = max(u for u in range(1, 6) if leaves % u == 0)

    def over_leaves(body):
        def block(b, carry):
            for u in range(unroll):
                body(b * unroll + u)
            return carry
        lax.fori_loop(0, leaves // unroll, block, 0)

    def leaf_solve(i):
        fwd[i] = mm(dinv[i], rhs[i])

    over_leaves(leaf_solve)

    def leaf_term(k):
        copy_coup[k].wait()

        def block(b, acc):
            for u in range(unroll):
                i = b * unroll + u
                acc = acc + pat[k, i].astype(F32) * mm(coup[i, k], fwd[i])
            return acc

        terms[k] = lax.fori_loop(0, leaves // unroll, block, jnp.zeros(terms.shape[1:], F32))

    def flip(i):
        fwd_t[i] = fwd[i].T

    pl.semaphore_wait(barrier, count)

    for level in range(hub_level):

        @pl.when(owner(level))
        def _():
            own_mats[level] = tinv[0].astype(F32)
            for t, hub in enumerate(hubs(level)):
                mat_copy(level, level, t, hub).start()
                rhs_copy(level, t, hub).start()
            for k in reversed(range(level)):
                own_mats[k] = tcoup[0, k].astype(F32)
                for t, hub in enumerate(hubs(level)):
                    mat_copy(level, k, t, hub).start()

    for k in reversed(range(depth)):
        leaf_term(k)

        @pl.when(odd)
        def _():
            part_copy(k).start()

    @pl.when(odd)
    def _():
        over_leaves(flip)

    @pl.when(even)
    def _():
        slot_wait(0, last)
        y = mm(tinv[0], trhs[0] - (terms[last] + slots[0, last]))
        for k in reversed(range(last)):
            slot_wait(0, k)
            stage[k] = terms[k] + slots[0, k] + mm(tcoup[0, k], y)

            @pl.when(left)
            def _():
                up_copy(0, k).start()

            @pl.when(jnp.logical_not(left))
            def _():
                up_copy(1, k).start()

        y_t[...] = y.T
        over_leaves(flip)

    @pl.when(is_hub)
    def _():
        def rest(k):
            slot_wait(0, k)
            slot_wait(1, k)
            return slots[0, k] + slots[1, k]

        y = mm(tinv[0], trhs[0] - rest(hub_level))
        top = hub_level - 1
        for k in reversed(range(hub_level)):
            mine[top, k] = rest(k) + mm(tcoup[0, k], y)
            swap_copy(top, k).start()
        y_t[...] = y.T
        for level in reversed(range(hub_level)):
            for k in reversed(range(level + 1)):
                send(
                    own_mats.at[k], mats.at[level, k], mat_send.at[0, k], mat_sem.at[level, k], partner
                ).wait_recv()
            send(
                trhs.at[0], high_rhs.at[level], mat_send.at[0, hub_level], rhs_sem.at[level], partner
            ).wait_recv()
            swap_copy(level, level).wait_recv()
            y = mm(mats[level, level], high_rhs[level] - (mine[level, level] + theirs[level, level]))
            for k in reversed(range(level)):
                swap_copy(level, k).wait_recv()
                mine[level - 1, k] = mine[level, k] + theirs[level, k] + mm(mats[level, k], y)
                swap_copy(level - 1, k).start()
            high_y[level] = y.T

        for level in range(hub_level + 1):
            own = level == hub_level
            value = y_t[...] if own else high_y[level]
            for k in range(level):
                value = value - mm(high_x[k], tcoup[0, k] if own else mats[level, k])
            high_x[level] = mm(value, tinv[0] if own else mats[level, level])
            down_copy(high_x.at[level], 1, level, me + 1).start()
            down_copy(high_x.at[level], 0, level, me - 1).start()
        top_out[0] = high_x[hub_level].T

    def leaf_back(k):
        x = path[k].astype(BF16)

        def body(i):
            value = fwd_t[i] - pat[k, i].astype(F32) * mm(x, coup[i, k])
            if k < last:
                fwd_t[i] = value
            else:
                out[i] = mm(value, dinv[i]).T
                pltpu.make_async_copy(out.at[i], sol_hbm.at[i], out_sem.at[i]).start()

        over_leaves(body)

    @pl.when(even)
    def _():
        for k in range(last):
            path_wait(k)
            pair_copy(k).start()
            y_t[...] = y_t[...] - mm(path[k], tcoup[0, k])
            if k + 1 == last:
                path[last] = mm(y_t[...], tinv[0])
                pair_copy(last).start()
            leaf_back(k)
        top_out[0] = path[last].T

    @pl.when(odd)
    def _():
        for k in range(last):
            path_wait(k)
            leaf_back(k)
        path_wait(last)

    for level in range(hub_level):

        @pl.when(owner(level))
        def _():
            top_out[0] = path[level].T

    @pl.when(me == (1 << depth) - 1)
    def _():
        top_out[0] = path[0].T

    copy_top = pltpu.make_async_copy(top_out, top_hbm, top_sem)
    copy_top.start()
    leaf_back(last)

    @pl.when(odd)
    def _():
        for k in range(depth):
            part_copy(k).wait_send()

    @pl.when(even)
    def _():
        for k in range(last):
            up_copy(0, k).wait_send()
        for k in range(depth):
            pair_copy(k).wait_send()

    @pl.when(is_hub)
    def _():
        for level in range(hub_level):
            for k in range(level + 1):
                swap_copy(level, k).wait_send()
        for k in range(hub_level + 1):
            down_copy(high_x.at[k], 0, k, partner).wait_send()
            down_copy(high_x.at[k], 1, k, partner).wait_send()

    for level in range(hub_level):

        @pl.when(owner(level))
        def _():
            for t, hub in enumerate(hubs(level)):
                rhs_copy(level, t, hub).wait_send()
                for k in range(level + 1):
                    mat_copy(level, k, t, hub).wait_send()

    copy_top.wait()

    def out_wait(i):
        pltpu.make_async_copy(out.at[i], sol_hbm.at[i], out_sem.at[i]).wait()

    over_leaves(out_wait)


def local(leaf_right_hand, leaf_diagonal_inverse, leaf_coupling, leaf_pattern, top_rhs, top_inverse, top_coupling):
    depth = lax.axis_size("col").bit_length() - 1
    high = depth - 2
    leaves, width, right = leaf_right_hand.shape
    tall, flat = (width, right), (right, width)
    anywhere = pl.BlockSpec(memory_space=pl.ANY)
    sem = pltpu.SemaphoreType.DMA
    return pl.pallas_call(
        functools.partial(kernel, depth),
        out_shape=(
            jax.ShapeDtypeStruct(leaf_right_hand.shape, F32),
            jax.ShapeDtypeStruct(top_rhs.shape, F32),
        ),
        in_specs=[anywhere] * 3 + [pl.BlockSpec(memory_space=pltpu.SMEM)] + [anywhere] * 3,
        out_specs=(anywhere, anywhere),
        scratch_shapes=[
            pltpu.VMEM(leaf_right_hand.shape, F32),
            pltpu.VMEM(leaf_diagonal_inverse.shape, BF16),
            pltpu.VMEM(leaf_coupling.shape, BF16),
            pltpu.VMEM(top_rhs.shape, F32),
            pltpu.VMEM(top_inverse.shape, BF16),
            pltpu.VMEM(top_coupling.shape, BF16),
            pltpu.VMEM((leaves, *tall), F32),
            pltpu.VMEM((leaves, *flat), F32),
            pltpu.VMEM((leaves, *tall), F32),
            pltpu.VMEM((1, *tall), F32),
            pltpu.VMEM((depth, *tall), F32),
            pltpu.VMEM((2, depth, *tall), F32),
            pltpu.VMEM((depth, *tall), F32),
            pltpu.VMEM((depth, *flat), F32),
            pltpu.VMEM(flat, F32),
            pltpu.VMEM((high, width, width), F32),
            pltpu.VMEM((high, high, width, width), F32),
            pltpu.VMEM((high, *tall), F32),
            pltpu.VMEM((high, high, *tall), F32),
            pltpu.VMEM((high, high, *tall), F32),
            pltpu.VMEM((high, *flat), F32),
            pltpu.VMEM((high + 1, *flat), F32),
            sem((2,)), sem((depth,)), sem((3,)), sem((leaves,)), sem,
            sem((2, depth)), sem((depth,)), sem((depth,)), sem((depth,)), sem((2, depth)),
            sem((1 << high, high + 1)), sem((high, high)), sem((high,)), sem((high, high)), sem((high, high)),
        ],
        compiler_params=pltpu.CompilerParams(
            collective_id=0, has_side_effects=True, vmem_limit_bytes=56 * 2**20
        ),
    )(leaf_right_hand, leaf_diagonal_inverse, leaf_coupling, leaf_pattern.T, top_rhs, top_inverse, top_coupling)


def solution(mesh):
    both = ("grp", "col")
    three, four = P(both, None, None), P(both, None, None, None)
    in_specs = (three, three, four, P(both, None), three, three, four)
    return jax.shard_map(local, mesh=mesh, in_specs=in_specs, out_specs=(three, three), check_vma=False)
```

time: 46.9 us -> 45.1 us (0.962)
  local copies, waits for them, and re-layouts: 4.53 us -> 3.17 us
    unnamed x5 -> x4, local copies, waits for them, and re-layouts: 4.53 us -> 3.17 us
where the time goes in v2:
time: 45.1 us; the launch traced here: 44.9 us
  Pallas kernels  41.1 us (91%)
  local copies, waits for them, and re-layouts  3.17 us (7%)
  between operations  0.65 us (1%)
    pallas_call x1, Pallas kernels, local(): pl.pallas_call(functools.partial(kernel, depth), out_shape=(jax.ShapeDtyp...  41.1 us
    unnamed x4, local copies, waits for them, and re-layouts  3.17 us

profile of v2, /device:TPU:7, one launch (start us, length us, event | category | flops | bytes accessed | tf_op | source)
XLA Modules:
  0.0 44.9 jit_solution(17919868963074353008)
XLA Ops:
  0.6 41.1 %shard_map.86 = (f32[10,256,128]{2,1,0:T(8,128)}, f32[1,256,128]{2,1,0:T(8,128)}) custom-call(f32[10,256,128]{2,1,0:T(8,128)} %rhs_hbm.1, bf16[10,256,256]{2,1,0:T(8,128)(2,1)} %dinv_hbm.1, bf16[10,4,256,256]{3,2,1,0:T(8,128)(2,1)} %coup_hbm.1, s32[4,10]{1,0:T(4,128)} %bitcast.1, f32[1,256,128]{2,1,0:T(8,128)} %trhs_hbm.1, bf16[1,256,256]{2,1,0:T(8,128)(2,1)} %tinv_hbm.1, ...), custom_call_target="tpu_custom_call" | custom-call | tf_op jit(solution)/shard_map/pallas_call | solution.py:342
  41.7 0.0 copy-start
  41.7 2.5 %copy.11 = f32[10,256,128]{2,1,0:T(8,128)} copy(f32[10,256,128]{2,1,0:T(8,128)} %get-tuple-element.4) | data formatting | bytes 2621440
  44.2 0.0 copy-done
  44.2 0.7 %copy.12 = f32[1,256,128]{2,1,0:T(8,128)} copy(f32[1,256,128]{2,1,0:T(8,128)S(1)} %copy-done) | data formatting | bytes 262144
Async XLA Ops:
  41.7 2.5 %copy-start = (f32[1,256,128]{2,1,0:T(8,128)S(1)}, f32[1,256,128]{2,1,0:T(8,128)}, u32[]{:S(2)}) copy-start(f32[1,256,128]{2,1,0:T(8,128)} %get-tuple-element.5) | copy-start | bytes 393220

commit v3 on v2

--- a/solution.py
+++ b/solution.py
@@ -20,14 +20,15 @@
     sol_hbm, top_hbm,
     rhs, dinv, coup, trhs, tinv, tcoup, fwd, fwd_t, out, top_out,
     terms, slots, stage, path, y_t,
-    own_mats, mats, high_rhs, mine, theirs, high_y, high_x,
+    own_mats, mats, mine, theirs, high_y, high_x,
     in_sem, coup_sem, tin_sem, out_sem, top_sem,
     slot_sem, path_sem, part_send, up_send, down_send,
-    mat_send, mat_sem, rhs_sem, swap_send, swap_sem,
+    mat_send, mat_sem, tip_sem, swap_send, swap_sem,
 ):
     leaves = rhs.shape[0]
     last = depth - 1
     hub_level = depth - 2
+    half = tinv.shape[1] // 2
     me = lax.axis_index("col")
     even = lax.rem(me, 2) == 0
     odd = lax.rem(me, 2) == 1
@@ -40,13 +41,13 @@
         span = 1 << (depth - level)
         return lax.rem(me, span) == span // 2 - 1
 
-    def hubs(level):
+    def entry(level):
         span = 1 << (depth - level)
-        return [me + 1 - span // 2 + 4 * t + 1 for t in range(span // 4)]
-
-    def owner_of(level):
-        span = 1 << (depth - level)
-        return me // span * span + span // 2 - 1
+        return me // span * span + span // 2 - 3
+
+    def others(level):
+        first = 1 << (depth - level - 3)
+        return [(t, me + 4 * (t + 1 - first)) for t in range(2 * first) if t + 1 != first]
 
     def opposite(level):
         step = 4 << (hub_level - 1 - level)
@@ -85,18 +86,28 @@
         greet(me - 1)
         greet(me + 1)
         for level in range(hub_level):
-            greet(owner_of(level))
             greet(opposite(level))
-
-    count = 1 + jnp.where(even, 1, 0) + jnp.where(is_hub, 2 + 2 * hub_level, 0)
+            here = me == entry(level)
+
+            @pl.when(here)
+            def _():
+                greet(me + 2)
+                for _t, hub in others(level):
+                    greet(hub)
+
+            @pl.when(jnp.logical_not(here))
+            def _():
+                greet(entry(level))
+
+    count = 1 + jnp.where(even, 1, 0) + jnp.where(is_hub, 2 + hub_level, 0)
     for level in range(hub_level):
 
         @pl.when(owner(level))
         def _():
-            for hub in hubs(level):
-                greet(hub)
-
-        count = count + jnp.where(owner(level), 1 << (hub_level - level), 0)
+            greet(me - 2)
+
+        hub_count = jnp.where(me == entry(level), 1 << (hub_level - level), 1)
+        count = count + jnp.where(owner(level), 1, 0) + jnp.where(is_hub, hub_count, 0)
 
     def send(src, dst, send_sem, recv_sem, device):
         return pltpu.make_async_remote_copy(
@@ -119,11 +130,23 @@
     def swap_copy(level, k):
         return send(mine.at[level, k], theirs.at[level, k], swap_send.at[level, k], swap_sem.at[level, k], opposite(level))
 
-    def mat_copy(level, k, t, hub):
-        return send(own_mats.at[k], mats.at[level, k], mat_send.at[t, k], mat_sem.at[level, k], hub)
-
-    def rhs_copy(level, t, hub):
-        return send(trhs.at[0], high_rhs.at[level], mat_send.at[t, hub_level], rhs_sem.at[level], hub)
+    def mat_parts(src, level, k, t, device):
+        dst, sems = mats.at[level, k], mat_send.at[level, t]
+        if k < level:
+            return [send(src, dst, sems.at[k], mat_sem.at[level, k], device)]
+        low, up = pl.ds(half, half), pl.ds(0, half)
+        return [
+            send(src.at[low], dst.at[low], sems.at[k], mat_sem.at[level, k], device),
+            send(src.at[up, up], dst.at[up, up], sems.at[hub_level], tip_sem.at[level], device),
+        ]
+
+    def own_parts(level, k):
+        return mat_parts(own_mats.at[k], level, k, 0, me - 2)
+
+    def mat_wait(level):
+        for k in range(level + 1):
+            for copy in mat_parts(mats.at[level, k], level, k, 0, partner):
+                copy.wait_recv()
 
     def slot_wait(side, k):
         send(slots.at[side, k], slots.at[side, k], part_send.at[k], slot_sem.at[side, k], partner).wait_recv()
@@ -134,6 +157,24 @@
     copy_tinv.wait()
     copy_trhs.wait()
     copy_tcoup.wait()
+    for level in range(hub_level):
+        mats[level, level, :half, half:] = jnp.zeros((half, half), F32)
+
+        @pl.when(owner(level))
+        def _():
+            for k in range(level + 1):
+                own_mats[k] = (tinv[0] if k == level else tcoup[0, k]).astype(F32)
+
+    pl.semaphore_wait(barrier, count)
+
+    for level in range(hub_level):
+
+        @pl.when(owner(level))
+        def _():
+            for k in reversed(range(level + 1)):
+                for copy in own_parts(level, k):
+                    copy.start()
+
     copy_dinv.wait()
     copy_rhs.wait()
     unroll = max(u for u in range(1, 6) if leaves % u == 0)
@@ -164,27 +205,27 @@
     def flip(i):
         fwd_t[i] = fwd[i].T
 
-    pl.semaphore_wait(barrier, count)
-
-    for level in range(hub_level):
-
-        @pl.when(owner(level))
-        def _():
-            own_mats[level] = tinv[0].astype(F32)
-            for t, hub in enumerate(hubs(level)):
-                mat_copy(level, level, t, hub).start()
-                rhs_copy(level, t, hub).start()
-            for k in reversed(range(level)):
-                own_mats[k] = tcoup[0, k].astype(F32)
-                for t, hub in enumerate(hubs(level)):
-                    mat_copy(level, k, t, hub).start()
-
     for k in reversed(range(depth)):
         leaf_term(k)
+        if k < hub_level:
+
+            @pl.when(owner(k))
+            def _():
+                terms[k] = terms[k] - trhs[0]
 
         @pl.when(odd)
         def _():
             part_copy(k).start()
+
+    for level in reversed(range(hub_level)):
+
+        @pl.when(jnp.logical_and(is_hub, me == entry(level)))
+        def _():
+            mat_wait(level)
+            for k in reversed(range(level + 1)):
+                for t, hub in others(level):
+                    for copy in mat_parts(mats.at[level, k], level, k, t, hub):
+                        copy.start()
 
     @pl.when(odd)
     def _():
@@ -223,15 +264,12 @@
             swap_copy(top, k).start()
         y_t[...] = y.T
         for level in reversed(range(hub_level)):
-            for k in reversed(range(level + 1)):
-                send(
-                    own_mats.at[k], mats.at[level, k], mat_send.at[0, k], mat_sem.at[level, k], partner
-                ).wait_recv()
-            send(
-                trhs.at[0], high_rhs.at[level], mat_send.at[0, hub_level], rhs_sem.at[level], partner
-            ).wait_recv()
+            @pl.when(me != entry(level))
+            def _():
+                mat_wait(level)
+
             swap_copy(level, level).wait_recv()
-            y = mm(mats[level, level], high_rhs[level] - (mine[level, level] + theirs[level, level]))
+            y = mm(mats[level, level], -(mine[level, level] + theirs[level, level]))
             for k in reversed(range(level)):
                 swap_copy(level, k).wait_recv()
                 mine[level - 1, k] = mine[level, k] + theirs[level, k] + mm(mats[level, k], y)
@@ -319,10 +357,16 @@
 
         @pl.when(owner(level))
         def _():
-            for t, hub in enumerate(hubs(level)):
-                rhs_copy(level, t, hub).wait_send()
-                for k in range(level + 1):
-                    mat_copy(level, k, t, hub).wait_send()
+            for k in range(level + 1):
+                for copy in own_parts(level, k):
+                    copy.wait_send()
+
+        @pl.when(jnp.logical_and(is_hub, me == entry(level)))
+        def _():
+            for k in range(level + 1):
+                for t, hub in others(level):
+                    for copy in mat_parts(mats.at[level, k], level, k, t, hub):
+                        copy.wait_send()
 
     copy_top.wait()
 
@@ -365,14 +409,13 @@
             pltpu.VMEM(flat, F32),
             pltpu.VMEM((high, width, width), F32),
             pltpu.VMEM((high, high, width, width), F32),
-            pltpu.VMEM((high, *tall), F32),
             pltpu.VMEM((high, high, *tall), F32),
             pltpu.VMEM((high, high, *tall), F32),
             pltpu.VMEM((high, *flat), F32),
             pltpu.VMEM((high + 1, *flat), F32),
             sem((2,)), sem((depth,)), sem((3,)), sem((leaves,)), sem,
             sem((2, depth)), sem((depth,)), sem((depth,)), sem((depth,)), sem((2, depth)),
-            sem((1 << high, high + 1)), sem((high, high)), sem((high,)), sem((high, high)), sem((high, high)),
+            sem((high, 1 << high, high + 1)), sem((high, high)), sem((high,)), sem((high, high)), sem((high, high)),
         ],
         compiler_params=pltpu.CompilerParams(
             collective_id=0, has_side_effects=True, vmem_limit_bytes=56 * 2**20

time: 45.1 us -> 40 us (0.89)
  the two profiles are of different devices: /device:TPU:7 before, /device:TPU:13 now
where the time goes in v3:
time: 40 us; the launch traced here: 39.8 us
  Pallas kernels  36 us (90%)
  local copies, waits for them, and re-layouts  3.17 us (8%)
  between operations  0.65 us (2%)
    pallas_call x1, Pallas kernels, local(): pl.pallas_call(functools.partial(kernel, depth), out_shape=(jax.ShapeDtyp...  36 us
    unnamed x4, local copies, waits for them, and re-layouts  3.17 us

profile of v3, /device:TPU:13, one launch (start us, length us, event | category | flops | bytes accessed | tf_op | source)
XLA Modules:
  0.0 39.8 jit_solution(6542355793336696341)
XLA Ops:
  0.6 36.0 %shard_map.86 = (f32[10,256,128]{2,1,0:T(8,128)}, f32[1,256,128]{2,1,0:T(8,128)}) custom-call(f32[10,256,128]{2,1,0:T(8,128)} %rhs_hbm.1, bf16[10,256,256]{2,1,0:T(8,128)(2,1)} %dinv_hbm.1, bf16[10,4,256,256]{3,2,1,0:T(8,128)(2,1)} %coup_hbm.1, s32[4,10]{1,0:T(4,128)} %bitcast.1, f32[1,256,128]{2,1,0:T(8,128)} %trhs_hbm.1, bf16[1,256,256]{2,1,0:T(8,128)(2,1)} %tinv_hbm.1, ...), custom_call_target="tpu_custom_call" | custom-call | tf_op jit(solution)/shard_map/pallas_call | solution.py:386
  36.6 0.0 copy-start
  36.6 2.5 %copy.11 = f32[10,256,128]{2,1,0:T(8,128)} copy(f32[10,256,128]{2,1,0:T(8,128)} %get-tuple-element.4) | data formatting | bytes 2621440
  39.1 0.0 copy-done
  39.1 0.7 %copy.12 = f32[1,256,128]{2,1,0:T(8,128)} copy(f32[1,256,128]{2,1,0:T(8,128)S(1)} %copy-done) | data formatting | bytes 262144
Async XLA Ops:
  36.6 2.5 %copy-start = (f32[1,256,128]{2,1,0:T(8,128)S(1)}, f32[1,256,128]{2,1,0:T(8,128)}, u32[]{:S(2)}) copy-start(f32[1,256,128]{2,1,0:T(8,128)} %get-tuple-element.5) | copy-start | bytes 393220
